TPU v7x, 32 devices: a whole 2x2x4 slice. The times are simulated.
32 devices in a mesh: dp: 8 (over z, x), expert: 4 (over y, core).
Axes of the slice: x: 2, y: 2, z: 4, core: 2. Of those that a mesh axis runs over, the one named last changes fastest.
Arguments:
- grads: bfloat16 [8, 4096, 3072], P('dp', None, 'expert'), parts along dimension 2, may hold values from -16 to 16
- error: bfloat16 [8, 4096, 3072], P('dp', None, 'expert'), parts along dimension 2, may hold values from -6 to 6
- q_start: float32 [3072, 32], P('expert'), parts along dimension 0, may hold values from -6 to 6
- bucket: float32 [8, 262144], P('dp', 'expert'), parts along dimension 1, may hold values from -6 to 6
Outputs:
- update: float32 [4096, 3072], P(None, 'expert'), parts along dimension 1
- new_error: bfloat16 [8, 4096, 3072], P('dp', None, 'expert'), parts along dimension 2
- bucket_mean: float32 [262144], P(('expert', 'dp')), parts along dimension 0
There are 4 independent parts, one for each index of `expert`. A program takes and returns all parts, laid end to end along the dimension named above; each array names one. Nothing has to cross between parts.
All inputs are finite; a program needn't handle non-finite values.
Results may differ from a plain program's by a relative error of at most 0.02.
Values may be sent and summed in bfloat16 or wider, within the bound.
No kernel may reach another device: no remote copies, remote signals or barrier semaphores. Data moves between devices by JAX's collectives and lax.ppermute only.
A program may use at most 128 MiB of HBM per device.

v0:
```python
import functools

import jax
import jax.numpy as jnp
from jax import lax
from jax.experimental import pallas as pl
from jax.experimental.pallas import tpu as pltpu
from jax.sharding import PartitionSpec as P

ITERS = 2
LANES = 128
SUBLANES = 8
MIB = 1024 * 1024
CONTRACT_LAST = (((1,), (1,)), ((), ()))


def exchange(chunks):
    return lax.all_to_all(chunks, "dp", split_axis=0, concat_axis=0, tiled=True)


def everywhere(share, size):
    return exchange(jnp.broadcast_to(share, (size,) + share.shape))


def three_parts(value):
    high = value.astype(jnp.bfloat16)
    rest = value - high.astype(jnp.float32)
    middle = rest.astype(jnp.bfloat16)
    low = (rest - middle.astype(jnp.float32)).astype(jnp.bfloat16)
    return high, middle, low


def pieces(rows, grow):
    sizes = [4 * LANES] * (rows // (4 * LANES))
    if grow:
        sizes[:1] = [LANES, LANES, 2 * LANES]
    return [(sum(sizes[:i]), size) for i, size in enumerate(sizes)]


def store_tiles(chunk, value):
    rank, columns = value.shape
    for tile in range(columns // LANES):
        chunk[tile * rank : (tile + 1) * rank, :] = value[:, tile * LANES : (tile + 1) * LANES]


def fine_product(left, right, axis):
    lh, lm, ll = three_parts(left)
    rh, rm, rl = three_parts(right)
    return lax.dot_general(
        jnp.concatenate([lh, lm, ll, lh, lm, lh], axis=axis),
        jnp.concatenate([rh, rh, rh, rm, rm, rl], axis=0),
        (((axis,), (0,)), ((), ())),
        preferred_element_type=jnp.float32,
    )


def first_kernel(replicas, flip, grads, error, q_start, compensated, outgoing, *scratch):
    landed, q_landed, sems, q_sem = scratch
    fetch_q = pltpu.make_async_copy(q_start, q_landed, q_sem)
    fetch_q.start()
    me = lax.axis_index("dp")
    half = replicas // 2
    block = grads.shape[0] // replicas
    starts, copies = [], []
    for k in range(half):
        starts.append(pl.multiple_of(((me >> 1) ^ k) * block, block))
        there = pl.multiple_of(((me & 1) ^ flip) * (half * block) + starts[k], block)
        for j, array in enumerate((grads, error)):
            copies.append(
                pltpu.make_async_copy(
                    array.at[pl.ds(there, block)], landed.at[j, k], sems.at[j, k]
                )
            )
            copies[-1].start(priority=j)
    fetch_q.wait()
    q_half = q_landed[...].astype(jnp.bfloat16)
    for k in range(half):
        copies[2 * k].wait()
        copies[2 * k + 1].wait()
        value = (landed[0, k].astype(jnp.float32) + landed[1, k].astype(jnp.float32)).astype(
            jnp.bfloat16
        )
        compensated[pl.ds(starts[k], block), :] = value
        local_p = lax.dot_general(q_half, value, CONTRACT_LAST, preferred_element_type=jnp.float32)
        store_tiles(outgoing.at[k], local_p.astype(jnp.bfloat16))


def first(grads, error, q_start, replicas, flip):
    rows, hidden = grads.shape
    rank = q_start.shape[0]
    block = rows // replicas
    half = replicas // 2
    return pl.pallas_call(
        functools.partial(first_kernel, replicas, flip),
        in_specs=[pl.BlockSpec(memory_space=pl.ANY)] * 3,
        out_specs=[pl.BlockSpec(memory_space=pltpu.VMEM)] * 2,
        out_shape=[
            pltpu.VMEM((half * block, hidden), jnp.bfloat16),
            pltpu.VMEM((half, block // LANES * rank, LANES), jnp.bfloat16),
        ],
        scratch_shapes=[
            pltpu.VMEM((2, half, block, hidden), jnp.bfloat16),
            pltpu.VMEM(q_start.shape, jnp.float32),
            pltpu.SemaphoreType.DMA((2, half)),
            pltpu.SemaphoreType.DMA(()),
        ],
        compiler_params=pltpu.CompilerParams(vmem_limit_bytes=53 * MIB),
        cost_estimate=pl.CostEstimate(
            flops=rows * hidden * rank, bytes_accessed=2 * rows * hidden, transcendentals=0
        ),
        name="compensate_and_left",
    )(grads, error, q_start)


def partner(value, by, size):
    return lax.ppermute(value, "dp", [(i, i ^ by) for i in range(size)])


def first_share(grads, error, q_start, replicas):
    other, theirs = first(grads, error, q_start, replicas, 1)
    arrived = partner(theirs, 1, replicas)
    own, mine = first(grads, error, q_start, replicas, 0)
    pairs = [
        arrived[k].astype(jnp.float32) + mine[k].astype(jnp.float32) for k in range(replicas // 2)
    ]
    total = pairs[0]
    for value in [
        partner(pairs[k].astype(jnp.bfloat16), 2 * k, replicas) for k in range(1, replicas // 2)
    ]:
        total = total + value.astype(jnp.float32)
    return (own, other), total


def inverse_lower(gram):
    rank = gram.shape[0]
    row = lax.broadcasted_iota(jnp.int32, (SUBLANES, 2 * rank), 0)
    across = lax.broadcasted_iota(jnp.int32, (SUBLANES, 2 * rank), 1)
    both = jnp.concatenate([jnp.zeros((rank, rank), jnp.float32), gram], axis=1)
    starts = range(0, rank, SUBLANES)
    tiles = [
        jnp.where(across == row + at, 1.0, both[at : at + SUBLANES, :]) for at in starts
    ]
    inverse = []
    for top, base in enumerate(starts):
        columns = [
            [
                jnp.broadcast_to(tile[:, rank + k : rank + k + 1], tile.shape)
                for tile in tiles[top:]
            ]
            for k in range(base, base + SUBLANES)
        ]
        for j in range(SUBLANES):
            head = columns[j][0]
            reciprocal = 1.0 / head[j : j + 1, :]
            pivot_row = tiles[top][j : j + 1, :]
            for at in range(len(columns[j])):
                factor = columns[j][at] * reciprocal
                if at == 0:
                    factor = jnp.where(row > j, factor, 0.0)
                for i in range(j + 1, SUBLANES):
                    columns[i][at] = columns[i][at] - factor * head[i : i + 1, :]
                tiles[top + at] = tiles[top + at] - factor * pivot_row
        done = tiles[top]
        pivots = jnp.sum(
            jnp.where(across == row + (rank + base), done, 0.0), axis=1, keepdims=True
        )
        inverse.append(done[:, :rank] * lax.rsqrt(pivots))
    return jnp.concatenate(inverse, axis=0)


def columns_of(arrived, tiles, x, first_tile, count):
    rank = arrived.shape[1] // tiles
    parts = []
    for at in range(first_tile, first_tile + count):
        block, tile = divmod(at, tiles)
        parts.append(arrived[2 * block + x, tile * rank : (tile + 1) * rank, :])
    return jnp.concatenate(parts, axis=1)


def right_kernel(tiles, arrived, halves, term, inverse_out=None):
    x = lax.axis_index("dp") & 1
    count = arrived.shape[0] // 2 * tiles
    factors = [columns_of(arrived, tiles, x ^ flip, 0, count) for flip in range(2)]
    factor_p = jnp.concatenate(factors, axis=1)
    gram = lax.dot_general(
        factor_p, factor_p, CONTRACT_LAST, preferred_element_type=jnp.float32
    )
    product = sum(
        jnp.dot(factor, half[...], preferred_element_type=jnp.float32)
        for factor, half in zip(factors, halves)
    )
    inverse = inverse_lower(gram)
    if inverse_out is not None:
        inverse_out[...] = inverse
    term[...] = fine_product(inverse, product, 1).astype(jnp.bfloat16)


def right(arrived, halves, rank, keep):
    out_shape = [pltpu.VMEM((rank, halves[0].shape[1]), jnp.bfloat16)]
    in_vmem = pl.BlockSpec(memory_space=pltpu.VMEM)
    if keep:
        out_shape.append(pltpu.VMEM((rank, rank), jnp.float32))
    return pl.pallas_call(
        functools.partial(right_kernel, arrived.shape[1] // rank),
        in_specs=[in_vmem, (in_vmem, in_vmem)],
        out_specs=[in_vmem] * len(out_shape),
        out_shape=out_shape,
        compiler_params=pltpu.CompilerParams(vmem_limit_bytes=24 * MIB),
        name="orthogonalize_and_right",
    )(arrived, halves)


def last_partner(value, step, size, detour):
    experts = lax.axis_size("expert")
    pairs = []
    for i in range(size):
        for e in range(experts):
            other = i ^ (step ^ 2 if detour and e % 2 else step)
            pairs.append((i * experts + e, other * experts + e))
    return lax.ppermute(value, ("dp", "expert"), pairs)


def addends(term, size, detour):
    one, two, three, four = [
        part.astype(jnp.float32) for part in [term] + [partner(term, by, size) for by in (1, 2, 3)]
    ]
    term = ((one + two) + (three + four)).astype(jnp.bfloat16)
    step = 4
    while 2 * step < size:
        term = (term.astype(jnp.float32) + partner(term, step, size).astype(jnp.float32)).astype(
            jnp.bfloat16
        )
        step *= 2
    return [term, last_partner(term, step, size, detour)]


def sum_of(parts):
    one, two = [part[...].astype(jnp.float32) for part in parts]
    return one + two


def left_kernel(parts, halves, bucket, outgoing, landed, sem):
    replicas = outgoing.shape[0]
    block = 2 * halves[0].shape[0] // replicas
    x = lax.axis_index("dp") & 1
    fetch = pltpu.make_async_copy(bucket, landed, sem)
    fetch.start()
    factor_q = sum_of(parts) / replicas
    scale = 1.0 / jnp.sqrt(jnp.sum(factor_q * factor_q, axis=1, keepdims=True) + 1e-06)
    q_half = factor_q.astype(jnp.bfloat16)
    for flip, half in enumerate(halves):
        for j in range(replicas // 2):
            local_p = lax.dot_general(
                q_half,
                half[j * block : (j + 1) * block, :],
                CONTRACT_LAST,
                preferred_element_type=jnp.float32,
            )
            store_tiles(outgoing.at[2 * j + (x ^ flip)], (local_p * scale).astype(jnp.bfloat16))
    fetch.wait()
    outgoing[:, -bucket.shape[1] :, :] = landed[...].astype(jnp.bfloat16)


def left(parts, halves, bucket):
    replicas = bucket.shape[0]
    tall = 2 * halves[0].shape[0] // replicas * parts[0].shape[0] // LANES + bucket.shape[1]
    in_vmem = pl.BlockSpec(memory_space=pltpu.VMEM)
    return pl.pallas_call(
        left_kernel,
        in_specs=[[in_vmem] * len(parts), (in_vmem, in_vmem), pl.BlockSpec(memory_space=pl.ANY)],
        out_specs=in_vmem,
        out_shape=pltpu.VMEM((replicas, tall, LANES), jnp.bfloat16),
        scratch_shapes=[pltpu.VMEM(bucket.shape, jnp.float32), pltpu.SemaphoreType.DMA(())],
        compiler_params=pltpu.CompilerParams(vmem_limit_bytes=24 * MIB),
        name="normalize_and_left",
    )(parts, halves, bucket)


def last_kernel(
    replicas, parts, inverse, arrived, halves, share,
    update, new_error, bucket_mean, update_held, error_held, sems, bucket_sem,
):
    tall = bucket_mean.shape[0]
    there = pl.ds(share.shape[0] - tall, tall)
    copies = [pltpu.make_async_copy(share.at[there], bucket_mean, bucket_sem)]
    copies[0].start()
    rows, hidden = halves[0].shape
    tiles = 2 * rows // replicas // LANES
    x = lax.axis_index("dp") & 1
    right = fine_product(inverse[...], sum_of(parts) / replicas, 0)
    right = jnp.concatenate(three_parts(right), axis=0)
    for flip, half in enumerate(halves):
        for i, (at, size) in enumerate(pieces(rows, flip == 0)):
            where = slice(at, at + size)
            p_block = columns_of(arrived, tiles, x ^ flip, at // LANES, size // LANES).T
            block = jnp.dot(
                jnp.concatenate([p_block] * 3, axis=1), right, preferred_element_type=jnp.float32
            )
            update_held[flip, where, :] = block
            error_held[flip, where, :] = (half[where, :].astype(jnp.float32) - block).astype(
                jnp.bfloat16
            )
            there = pl.ds(pl.multiple_of((x ^ flip) * rows + at, LANES), size)
            for j, (held, out) in enumerate(((update_held, update), (error_held, new_error))):
                copies.append(
                    pltpu.make_async_copy(
                        held.at[flip, pl.ds(at, size)], out.at[there], sems.at[j, flip, i]
                    )
                )
                copies[-1].start(priority=j)
    for copy in copies:
        copy.wait()


def last(parts, inverse, arrived, halves, share, replicas, bucket_tall):
    rows, hidden = halves[0].shape
    in_vmem = pl.BlockSpec(memory_space=pltpu.VMEM)
    return pl.pallas_call(
        functools.partial(last_kernel, replicas),
        in_specs=[[in_vmem] * len(parts), in_vmem, in_vmem, (in_vmem, in_vmem), in_vmem],
        out_specs=[pl.BlockSpec(memory_space=pl.ANY)] * 3,
        out_shape=[
            jax.ShapeDtypeStruct((2 * rows, hidden), jnp.float32),
            jax.ShapeDtypeStruct((2 * rows, hidden), jnp.bfloat16),
            jax.ShapeDtypeStruct((bucket_tall, LANES), jnp.float32),
        ],
        scratch_shapes=[
            pltpu.VMEM((2, rows, hidden), jnp.float32),
            pltpu.VMEM((2, rows, hidden), jnp.bfloat16),
            pltpu.SemaphoreType.DMA((2, 2, len(pieces(rows, True)))),
            pltpu.SemaphoreType.DMA(()),
        ],
        compiler_params=pltpu.CompilerParams(vmem_limit_bytes=40 * MIB),
        name="update_and_error",
    )(parts, inverse, arrived, halves, share)


def on_device(grads, error, q_start, bucket):
    replicas = lax.axis_size("dp")
    rows = grads.shape[1]
    rank = q_start.shape[1]
    bucket = bucket.reshape(replicas, -1, LANES)
    tall = rows // replicas * rank // LANES
    halves, share = first_share(grads[0], error[0], q_start.T, replicas)
    for step in range(ITERS):
        if step > 0:
            share = jnp.sum(exchange(outgoing).astype(jnp.float32), axis=0)
        share = share / replicas
        factor_p = everywhere(share[:tall].astype(jnp.bfloat16), replicas)
        term, *inverse = right(factor_p, halves, rank, step + 1 == ITERS)
        parts = addends(term, replicas, step + 1 < ITERS)
        if step + 1 < ITERS:
            outgoing = left(parts, halves, bucket)
    update, new_error, bucket_mean = last(
        parts, inverse[0], factor_p, halves, share, replicas, bucket.shape[1]
    )
    return (update, new_error[None], bucket_mean.reshape(-1))


def solution(mesh):
    return jax.shard_map(
        on_device,
        mesh=mesh,
        in_specs=(
            P("dp", None, "expert"),
            P("dp", None, "expert"),
            P("expert", None),
            P("dp", "expert"),
        ),
        out_specs=(P(None, "expert"), P("dp", None, "expert"), P(("expert", "dp"))),
        check_vma=False,
    )
```

profile of v0, /device:TPU:0, one launch (start us, length us, event | category | flops | bytes accessed | tf_op | source)
XLA Modules:
  0.0 89.5 jit_solution(16372477772173852806)
XLA Ops:
  0.6 3.6 %compensate_and_left.2 = (bf16[2048,768]{1,0:T(8,128)(2,1)S(1)}, bf16[4,128,128]{2,1,0:T(8,128)(2,1)S(1)}) custom-call(bf16[4096,768]{1,0:T(8,128)(2,1)} %bitcast.23, bf16[4096,768]{1,0:T(8,128)(2,1)} %bitcast.25, f32[32,768]{1,0:T(8,128)} %bitcast.27), custom_call_target="tpu_custom_call" | custom-call | flops 100663296 | bytes 6291456 | tf_op jit(solution)/shard_map/compensate_and_left/pallas_call | solution.py:93
  4.2 3.0 %collective-permute-start = (bf16[4,128,128]{2,1,0:T(8,128)(2,1)S(1)}, bf16[4,128,128]{2,1,0:T(8,128)(2,1)S(1)}, u32[]{:S(2)}, u32[]{:S(2)}) collective-permute-start(bf16[4,128,128]{2,1,0:T(8,128)(2,1)S(1)} %get-tuple-element.12), channel_id=1, source_target_pairs={{0,4},{4,0},{8,12},{12,8},{16,20},{20,16},{24,28},{28,24},{1,5},{5... | collective-permute-start | bytes 393224 | tf_op jit(solution)/shard_map/ppermute | solution.py:116
  7.3 3.6 %compensate_and_left.3 = (bf16[2048,768]{1,0:T(8,128)(2,1)S(1)}, bf16[4,128,128]{2,1,0:T(8,128)(2,1)S(1)}) custom-call(bf16[4096,768]{1,0:T(8,128)(2,1)} %bitcast.24, bf16[4096,768]{1,0:T(8,128)(2,1)} %bitcast.26, f32[32,768]{1,0:T(8,128)} %bitcast.28), custom_call_target="tpu_custom_call" | custom-call | flops 100663296 | bytes 6291456 | tf_op jit(solution)/shard_map/compensate_and_left/pallas_call | solution.py:93
  10.9 0.0 copy-start
  10.9 0.0 collective-permute-done
  10.9 1.8 %collective-permute-start.1 = (bf16[128,128]{1,0:T(8,128)(2,1)S(1)}, bf16[128,128]{1,0:T(8,128)(2,1)S(1)}, u32[]{:S(2)}, u32[]{:S(2)}) collective-permute-start(bf16[128,128]{1,0:T(8,128)(2,1)S(1)} %get-tuple-element.21), channel_id=1, source_target_pairs={{0,8},{4,12},{8,0},{12,4},{16,24},{20,28},{24,16},{28,20},{1,9},{5... | collective-permute-start | bytes 98312 | tf_op jit(solution)/shard_map/ppermute | solution.py:116
  12.7 2.5 %collective-permute-start.3 = (bf16[128,128]{1,0:T(8,128)(2,1)S(1)}, bf16[128,128]{1,0:T(8,128)(2,1)S(1)}, u32[]{:S(2)}, u32[]{:S(2)}) collective-permute-start(bf16[128,128]{1,0:T(8,128)(2,1)S(1)} %get-tuple-element.22), channel_id=1, source_target_pairs={{0,24},{4,28},{8,16},{12,20},{16,8},{20,12},{24,0},{28,4},{1,25},{... | collective-permute-start | bytes 98312 | tf_op jit(solution)/shard_map/ppermute | solution.py:116
  15.1 0.1 collective-permute-start.2
  15.3 0.0 collective-permute-done.1
  15.3 3.2 %collective-permute-done.3 = bf16[128,128]{1,0:T(8,128)(2,1)S(1)} collective-permute-done((bf16[128,128]{1,0:T(8,128)(2,1)S(1)}, bf16[128,128]{1,0:T(8,128)(2,1)S(1)}, u32[]{:S(2)}, u32[]{:S(2)}) %collective-permute-start.3) | collective-permute-done | bytes 32800 | tf_op jit(solution)/shard_map/ppermute | solution.py:116
  18.4 1.9 %collective-permute-done.2 = bf16[128,128]{1,0:T(8,128)(2,1)S(1)} collective-permute-done((bf16[128,128]{1,0:T(8,128)(2,1)S(1)}, bf16[128,128]{1,0:T(8,128)(2,1)S(1)}, u32[]{:S(2)}, u32[]{:S(2)}) %collective-permute-start.2) | collective-permute-done | bytes 32800 | tf_op jit(solution)/shard_map/ppermute | solution.py:116
  20.4 11.5 %all_to_all.15.arrived = bf16[8,128,128]{2,1,0:T(8,128)(2,1)S(1)} all-to-all(bf16[8,128,128]{2,1,0:T(8,128)(2,1)S(1)} %broadcast_in_dim.9), channel_id=1, replica_groups=mesh['dp'=8,'expert'=4] {'dp'}, dimensions={0} | all-to-all | bytes 524288 | tf_op jit(solution)/shard_map/all_to_all | solution.py:18
  31.9 1.4 %orthogonalize_and_right.2 = bf16[32,768]{1,0:T(8,128)(2,1)S(1)} custom-call(bf16[8,128,128]{2,1,0:T(8,128)(2,1)S(1)} %all_to_all.15.arrived, bf16[2048,768]{1,0:T(8,128)(2,1)S(1)} %get-tuple-element.14.halves_0_, bf16[2048,768]{1,0:T(8,128)(2,1)S(1)} %get-tuple-element.15.halves_1_), custom_call_target="tpu_custom_call" | custom-call | tf_op jit(solution)/shard_map/orthogonalize_and_right/pallas_call | solution.py:203
  33.3 1.0 %collective-permute-start.6 = (bf16[32,768]{1,0:T(8,128)(2,1)S(1)}, bf16[32,768]{1,0:T(8,128)(2,1)S(1)}, u32[]{:S(2)}, u32[]{:S(2)}) collective-permute-start(bf16[32,768]{1,0:T(8,128)(2,1)S(1)} %orthogonalize_and_right.2), channel_id=1, source_target_pairs={{0,12},{4,8},{8,4},{12,0},{16,28},{20,24},{24,20},{28,16},{1,13},{... | collective-permute-start | bytes 147464 | tf_op jit(solution)/shard_map/ppermute | solution.py:116
  34.3 0.6 collective-permute-start.5
  34.8 2.0 %collective-permute-start.4 = (bf16[32,768]{1,0:T(8,128)(2,1)S(1)}, bf16[32,768]{1,0:T(8,128)(2,1)S(1)}, u32[]{:S(2)}, u32[]{:S(2)}) collective-permute-start(bf16[32,768]{1,0:T(8,128)(2,1)S(1)} %orthogonalize_and_right.2), channel_id=1, source_target_pairs={{0,4},{4,0},{8,12},{12,8},{16,20},{20,16},{24,28},{28,24},{1,5},{5... | collective-permute-start | bytes 147464 | tf_op jit(solution)/shard_map/ppermute | solution.py:116
  36.8 1.5 %collective-permute-done.6 = bf16[32,768]{1,0:T(8,128)(2,1)S(1)} collective-permute-done((bf16[32,768]{1,0:T(8,128)(2,1)S(1)}, bf16[32,768]{1,0:T(8,128)(2,1)S(1)}, u32[]{:S(2)}, u32[]{:S(2)}) %collective-permute-start.6) | collective-permute-done | bytes 49184 | tf_op jit(solution)/shard_map/ppermute | solution.py:116
  38.3 0.0 collective-permute-done.5
  38.4 0.6 collective-permute-done.4
  39.0 1.2 %collective-permute-start.7 = (bf16[32,768]{1,0:T(8,128)(2,1)S(1)}, bf16[32,768]{1,0:T(8,128)(2,1)S(1)}, u32[]{:S(2)}, u32[]{:S(2)}) collective-permute-start(bf16[32,768]{1,0:T(8,128)(2,1)S(1)} %add_convert_fusion.1.parts_0_), channel_id=1, source_target_pairs={{0,16},{1,25},{2,18},{3,27},{4,20},{5,29},{6,22},{7,31},{8,24},{9,... | collective-permute-start | bytes 147464 | tf_op jit(solution)/shard_map/ppermute | solution.py:220
  40.1 3.9 %collective-permute-done.7.parts_1_ = bf16[32,768]{1,0:T(8,128)(2,1)S(1)} collective-permute-done((bf16[32,768]{1,0:T(8,128)(2,1)S(1)}, bf16[32,768]{1,0:T(8,128)(2,1)S(1)}, u32[]{:S(2)}, u32[]{:S(2)}) %collective-permute-start.7) | collective-permute-done | bytes 49184 | tf_op jit(solution)/shard_map/ppermute | solution.py:220
  44.0 0.0 copy-done
  44.0 2.0 %normalize_and_left.1 = bf16[8,192,128]{2,1,0:T(8,128)(2,1)S(1)} custom-call(bf16[32,768]{1,0:T(8,128)(2,1)S(1)} %add_convert_fusion.1.parts_0_, bf16[32,768]{1,0:T(8,128)(2,1)S(1)} %collective-permute-done.7.parts_1_, bf16[2048,768]{1,0:T(8,128)(2,1)S(1)} %get-tuple-element.14.halves_0_, bf16[2048,768]{1,0:T(8,128)(2,1)S(1)} %get-tuple-element.15.halves_1_, ...), custom_call_target="tpu_custom_call" | custom-call | tf_op jit(solution)/shard_map/normalize_and_left/pallas_call | solution.py:268
  46.0 13.1 %all_to_all.16 = bf16[8,192,128]{2,1,0:T(8,128)(2,1)S(1)} all-to-all(bf16[8,192,128]{2,1,0:T(8,128)(2,1)S(1)} %normalize_and_left.1), channel_id=1, replica_groups=mesh['dp'=8,'expert'=4] {'dp'}, dimensions={0} | all-to-all | bytes 786432 | tf_op jit(solution)/shard_map/all_to_all | solution.py:18
  59.1 0.1 convert_reduce_fusion
  59.2 11.1 %all_to_all.17.arrived = bf16[8,128,128]{2,1,0:T(8,128)(2,1)S(1)} all-to-all(bf16[8,128,128]{2,1,0:T(8,128)(2,1)S(1)} %broadcast_in_dim.10), channel_id=1, replica_groups=mesh['dp'=8,'expert'=4] {'dp'}, dimensions={0} | all-to-all | bytes 524288 | tf_op jit(solution)/shard_map/all_to_all | solution.py:18
  70.3 1.4 %orthogonalize_and_right.3 = (bf16[32,768]{1,0:T(8,128)(2,1)S(1)}, f32[32,32]{1,0:T(8,128)S(1)}) custom-call(bf16[8,128,128]{2,1,0:T(8,128)(2,1)S(1)} %all_to_all.17.arrived, bf16[2048,768]{1,0:T(8,128)(2,1)S(1)} %get-tuple-element.14.halves_0_, bf16[2048,768]{1,0:T(8,128)(2,1)S(1)} %get-tuple-element.15.halves_1_), custom_call_target="tpu_custom_call" | custom-call | tf_op jit(solution)/shard_map/orthogonalize_and_right/pallas_call | solution.py:203
  71.7 1.0 %collective-permute-start.10 = (bf16[32,768]{1,0:T(8,128)(2,1)S(1)}, bf16[32,768]{1,0:T(8,128)(2,1)S(1)}, u32[]{:S(2)}, u32[]{:S(2)}) collective-permute-start(bf16[32,768]{1,0:T(8,128)(2,1)S(1)} %get-tuple-element.16), channel_id=1, source_target_pairs={{0,12},{4,8},{8,4},{12,0},{16,28},{20,24},{24,20},{28,16},{1,13},{... | collective-permute-start | bytes 147464 | tf_op jit(solution)/shard_map/ppermute | solution.py:116
  72.7 0.6 collective-permute-start.9
  73.2 2.0 %collective-permute-start.8 = (bf16[32,768]{1,0:T(8,128)(2,1)S(1)}, bf16[32,768]{1,0:T(8,128)(2,1)S(1)}, u32[]{:S(2)}, u32[]{:S(2)}) collective-permute-start(bf16[32,768]{1,0:T(8,128)(2,1)S(1)} %get-tuple-element.16), channel_id=1, source_target_pairs={{0,4},{4,0},{8,12},{12,8},{16,20},{20,16},{24,28},{28,24},{1,5},{5... | collective-permute-start | bytes 147464 | tf_op jit(solution)/shard_map/ppermute | solution.py:116
  75.3 1.5 %collective-permute-done.10 = bf16[32,768]{1,0:T(8,128)(2,1)S(1)} collective-permute-done((bf16[32,768]{1,0:T(8,128)(2,1)S(1)}, bf16[32,768]{1,0:T(8,128)(2,1)S(1)}, u32[]{:S(2)}, u32[]{:S(2)}) %collective-permute-start.10) | collective-permute-done | bytes 49184 | tf_op jit(solution)/shard_map/ppermute | solution.py:116
  76.8 0.0 collective-permute-done.9
  76.8 0.6 collective-permute-done.8
  77.4 1.3 %collective-permute-start.11 = (bf16[32,768]{1,0:T(8,128)(2,1)S(1)}, bf16[32,768]{1,0:T(8,128)(2,1)S(1)}, u32[]{:S(2)}, u32[]{:S(2)}) collective-permute-start(bf16[32,768]{1,0:T(8,128)(2,1)S(1)} %add_convert_fusion.parts_0_), channel_id=1, source_target_pairs={{0,16},{1,17},{2,18},{3,19},{4,20},{5,21},{6,22},{7,23},{8,24},{9,... | collective-permute-start | bytes 147464 | tf_op jit(solution)/shard_map/ppermute | solution.py:220
  78.7 3.7 %collective-permute-done.11.parts_1_ = bf16[32,768]{1,0:T(8,128)(2,1)S(1)} collective-permute-done((bf16[32,768]{1,0:T(8,128)(2,1)S(1)}, bf16[32,768]{1,0:T(8,128)(2,1)S(1)}, u32[]{:S(2)}, u32[]{:S(2)}) %collective-permute-start.11) | collective-permute-done | bytes 49184 | tf_op jit(solution)/shard_map/ppermute | solution.py:220
  82.4 7.1 %update_and_error.1 = (f32[4096,768]{1,0:T(8,128)}, bf16[4096,768]{1,0:T(8,128)(2,1)}, f32[64,128]{1,0:T(8,128)}) custom-call(bf16[32,768]{1,0:T(8,128)(2,1)S(1)} %add_convert_fusion.parts_0_, bf16[32,768]{1,0:T(8,128)(2,1)S(1)} %collective-permute-done.11.parts_1_, f32[32,32]{1,0:T(8,128)S(1)} %get-tuple-element.17.inverse, ...), custom_call_target="tpu_custom_call" | custom-call | tf_op jit(solution)/shard_map/update_and_error/pallas_call | solution.py:318
  (8 shorter events, 0.2 us)
Async XLA Ops:
  4.2 6.6 %collective-permute-start = (bf16[4,128,128]{2,1,0:T(8,128)(2,1)S(1)}, bf16[4,128,128]{2,1,0:T(8,128)(2,1)S(1)}, u32[]{:S(2)}, u32[]{:S(2)}) collective-permute-start(bf16[4,128,128]{2,1,0:T(8,128)(2,1)S(1)} %get-tuple-element.12), channel_id=1, source_target_pairs={{0,4},{4,0},{8,12},{12,8},{16,20},{20,16},{24,28},{28,24},{1,5},{5... | collective-permute-start | bytes 393224 | tf_op jit(solution)/shard_map/ppermute | solution.py:116
  10.9 33.2 %copy-start = (f32[1,65536]{1,0:T(1,128)S(1)}, f32[1,65536]{1,0:T(1,128)}, u32[]{:S(2)}) copy-start(f32[1,65536]{1,0:T(1,128)} %param.7) | copy-start | bytes 786436
  10.9 4.4 %collective-permute-start.1 = (bf16[128,128]{1,0:T(8,128)(2,1)S(1)}, bf16[128,128]{1,0:T(8,128)(2,1)S(1)}, u32[]{:S(2)}, u32[]{:S(2)}) collective-permute-start(bf16[128,128]{1,0:T(8,128)(2,1)S(1)} %get-tuple-element.21), channel_id=1, source_target_pairs={{0,8},{4,12},{8,0},{12,4},{16,24},{20,28},{24,16},{28,20},{1,9},{5... | collective-permute-start | bytes 98312 | tf_op jit(solution)/shard_map/ppermute | solution.py:116
  12.7 5.8 %collective-permute-start.3 = (bf16[128,128]{1,0:T(8,128)(2,1)S(1)}, bf16[128,128]{1,0:T(8,128)(2,1)S(1)}, u32[]{:S(2)}, u32[]{:S(2)}) collective-permute-start(bf16[128,128]{1,0:T(8,128)(2,1)S(1)} %get-tuple-element.22), channel_id=1, source_target_pairs={{0,24},{4,28},{8,16},{12,20},{16,8},{20,12},{24,0},{28,4},{1,25},{... | collective-permute-start | bytes 98312 | tf_op jit(solution)/shard_map/ppermute | solution.py:116
  15.1 5.2 %collective-permute-start.2 = (bf16[128,128]{1,0:T(8,128)(2,1)S(1)}, bf16[128,128]{1,0:T(8,128)(2,1)S(1)}, u32[]{:S(2)}, u32[]{:S(2)}) collective-permute-start(bf16[128,128]{1,0:T(8,128)(2,1)S(1)} %get-tuple-element.23), channel_id=1, source_target_pairs={{0,16},{4,20},{8,24},{12,28},{16,0},{20,4},{24,8},{28,12},{1,17},{... | collective-permute-start | bytes 98312 | tf_op jit(solution)/shard_map/ppermute | solution.py:116
  33.3 5.1 %collective-permute-start.6 = (bf16[32,768]{1,0:T(8,128)(2,1)S(1)}, bf16[32,768]{1,0:T(8,128)(2,1)S(1)}, u32[]{:S(2)}, u32[]{:S(2)}) collective-permute-start(bf16[32,768]{1,0:T(8,128)(2,1)S(1)} %orthogonalize_and_right.2), channel_id=1, source_target_pairs={{0,12},{4,8},{8,4},{12,0},{16,28},{20,24},{24,20},{28,16},{1,13},{... | collective-permute-start | bytes 147464 | tf_op jit(solution)/shard_map/ppermute | solution.py:116
  34.3 4.1 %collective-permute-start.5 = (bf16[32,768]{1,0:T(8,128)(2,1)S(1)}, bf16[32,768]{1,0:T(8,128)(2,1)S(1)}, u32[]{:S(2)}, u32[]{:S(2)}) collective-permute-start(bf16[32,768]{1,0:T(8,128)(2,1)S(1)} %orthogonalize_and_right.2), channel_id=1, source_target_pairs={{0,8},{4,12},{8,0},{12,4},{16,24},{20,28},{24,16},{28,20},{1,9},{5... | collective-permute-start | bytes 147464 | tf_op jit(solution)/shard_map/ppermute | solution.py:116
  34.8 4.1 %collective-permute-start.4 = (bf16[32,768]{1,0:T(8,128)(2,1)S(1)}, bf16[32,768]{1,0:T(8,128)(2,1)S(1)}, u32[]{:S(2)}, u32[]{:S(2)}) collective-permute-start(bf16[32,768]{1,0:T(8,128)(2,1)S(1)} %orthogonalize_and_right.2), channel_id=1, source_target_pairs={{0,4},{4,0},{8,12},{12,8},{16,20},{20,16},{24,28},{28,24},{1,5},{5... | collective-permute-start | bytes 147464 | tf_op jit(solution)/shard_map/ppermute | solution.py:116
  39.0 5.1 %collective-permute-start.7 = (bf16[32,768]{1,0:T(8,128)(2,1)S(1)}, bf16[32,768]{1,0:T(8,128)(2,1)S(1)}, u32[]{:S(2)}, u32[]{:S(2)}) collective-permute-start(bf16[32,768]{1,0:T(8,128)(2,1)S(1)} %add_convert_fusion.1.parts_0_), channel_id=1, source_target_pairs={{0,16},{1,25},{2,18},{3,27},{4,20},{5,29},{6,22},{7,31},{8,24},{9,... | collective-permute-start | bytes 147464 | tf_op jit(solution)/shard_map/ppermute | solution.py:220
  71.7 5.1 %collective-permute-start.10 = (bf16[32,768]{1,0:T(8,128)(2,1)S(1)}, bf16[32,768]{1,0:T(8,128)(2,1)S(1)}, u32[]{:S(2)}, u32[]{:S(2)}) collective-permute-start(bf16[32,768]{1,0:T(8,128)(2,1)S(1)} %get-tuple-element.16), channel_id=1, source_target_pairs={{0,12},{4,8},{8,4},{12,0},{16,28},{20,24},{24,20},{28,16},{1,13},{... | collective-permute-start | bytes 147464 | tf_op jit(solution)/shard_map/ppermute | solution.py:116
  72.7 4.1 %collective-permute-start.9 = (bf16[32,768]{1,0:T(8,128)(2,1)S(1)}, bf16[32,768]{1,0:T(8,128)(2,1)S(1)}, u32[]{:S(2)}, u32[]{:S(2)}) collective-permute-start(bf16[32,768]{1,0:T(8,128)(2,1)S(1)} %get-tuple-element.16), channel_id=1, source_target_pairs={{0,8},{4,12},{8,0},{12,4},{16,24},{20,28},{24,16},{28,20},{1,9},{5... | collective-permute-start | bytes 147464 | tf_op jit(solution)/shard_map/ppermute | solution.py:116
  73.2 4.1 %collective-permute-start.8 = (bf16[32,768]{1,0:T(8,128)(2,1)S(1)}, bf16[32,768]{1,0:T(8,128)(2,1)S(1)}, u32[]{:S(2)}, u32[]{:S(2)}) collective-permute-start(bf16[32,768]{1,0:T(8,128)(2,1)S(1)} %get-tuple-element.16), channel_id=1, source_target_pairs={{0,4},{4,0},{8,12},{12,8},{16,20},{20,16},{24,28},{28,24},{1,5},{5... | collective-permute-start | bytes 147464 | tf_op jit(solution)/shard_map/ppermute | solution.py:116
  77.4 5.1 %collective-permute-start.11 = (bf16[32,768]{1,0:T(8,128)(2,1)S(1)}, bf16[32,768]{1,0:T(8,128)(2,1)S(1)}, u32[]{:S(2)}, u32[]{:S(2)}) collective-permute-start(bf16[32,768]{1,0:T(8,128)(2,1)S(1)} %add_convert_fusion.parts_0_), channel_id=1, source_target_pairs={{0,16},{1,17},{2,18},{3,19},{4,20},{5,21},{6,22},{7,23},{8,24},{9,... | collective-permute-start | bytes 147464 | tf_op jit(solution)/shard_map/ppermute | solution.py:220
where the time goes:
time: 89.7 us; the launch traced here: 89.5 us
  blocking collectives  35.6 us (40%)
  Pallas kernels  19.1 us (21%)
  starting transfers between devices  17 us (19%)
  waiting for transfers between devices  16.8 us (19%)
    all_to_all x3, blocking collectives, exchange(): return lax.all_to_all(chunks, 'dp', split_axis=0, concat_axis=0, tiled=True)  35.6 us
    ppermute x10, starting transfers between devices, partner(): return lax.ppermute(value, 'dp', [(i, i ^ by) for i in range(size)])  14.5 us
    ppermute x10, waiting for transfers between devices, partner(): return lax.ppermute(value, 'dp', [(i, i ^ by) for i in range(size)])  9.2 us
    ppermute x2, waiting for transfers between devices, last_partner(): return lax.ppermute(value, ('dp', 'expert'), pairs)  7.6 us
    pallas_call x2, Pallas kernels, first(): pl.pallas_call(functools.partial(first_kernel, replicas, flip), in_specs=...  7.21 us
    pallas_call x1, Pallas kernels, last(): pl.pallas_call(functools.partial(last_kernel, replicas), in_specs=[[in_vm...  7.09 us
    pallas_call x2, Pallas kernels, right(): pl.pallas_call(functools.partial(right_kernel, arrived.shape[1] // rank),...  2.86 us
    ppermute x2, starting transfers between devices, last_partner(): return lax.ppermute(value, ('dp', 'expert'), pairs)  2.51 us
  transfers between devices with their start and end apart: 12, of which 8 were waited for; matrix products, arithmetic and copies ran while one was open for 0% of the time, Pallas kernels for 4%

commit v1 on v0

--- a/solution.py
+++ b/solution.py
@@ -239,12 +239,11 @@
     return one + two
 
 
-def left_kernel(parts, halves, bucket, outgoing, landed, sem):
+def left_kernel(parts, halves, bucket, outgoing):
     replicas = outgoing.shape[0]
     block = 2 * halves[0].shape[0] // replicas
     x = lax.axis_index("dp") & 1
-    fetch = pltpu.make_async_copy(bucket, landed, sem)
-    fetch.start()
+    outgoing[:, -bucket.shape[1] :, :] = bucket[...].astype(jnp.bfloat16)
     factor_q = sum_of(parts) / replicas
     scale = 1.0 / jnp.sqrt(jnp.sum(factor_q * factor_q, axis=1, keepdims=True) + 1e-06)
     q_half = factor_q.astype(jnp.bfloat16)
@@ -257,8 +256,6 @@
                 preferred_element_type=jnp.float32,
             )
             store_tiles(outgoing.at[2 * j + (x ^ flip)], (local_p * scale).astype(jnp.bfloat16))
-    fetch.wait()
-    outgoing[:, -bucket.shape[1] :, :] = landed[...].astype(jnp.bfloat16)
 
 
 def left(parts, halves, bucket):
@@ -267,10 +264,9 @@
     in_vmem = pl.BlockSpec(memory_space=pltpu.VMEM)
     return pl.pallas_call(
         left_kernel,
-        in_specs=[[in_vmem] * len(parts), (in_vmem, in_vmem), pl.BlockSpec(memory_space=pl.ANY)],
+        in_specs=[[in_vmem] * len(parts), (in_vmem, in_vmem), in_vmem],
         out_specs=in_vmem,
         out_shape=pltpu.VMEM((replicas, tall, LANES), jnp.bfloat16),
-        scratch_shapes=[pltpu.VMEM(bucket.shape, jnp.float32), pltpu.SemaphoreType.DMA(())],
         compiler_params=pltpu.CompilerParams(vmem_limit_bytes=24 * MIB),
         name="normalize_and_left",
     )(parts, halves, bucket)

time: 89.7 us -> 89.7 us (level)
  no operation moved by 1% of the time
where the time goes in v1:
time: 89.7 us; the launch traced here: 89.5 us
  blocking collectives  35.6 us (40%)
  Pallas kernels  19.1 us (21%)
  starting transfers between devices  17 us (19%)
  waiting for transfers between devices  16.8 us (19%)
    all_to_all x3, blocking collectives, exchange(): return lax.all_to_all(chunks, 'dp', split_axis=0, concat_axis=0, tiled=True)  35.6 us
    ppermute x10, starting transfers between devices, partner(): return lax.ppermute(value, 'dp', [(i, i ^ by) for i in range(size)])  14.5 us
    ppermute x10, waiting for transfers between devices, partner(): return lax.ppermute(value, 'dp', [(i, i ^ by) for i in range(size)])  9.2 us
    ppermute x2, waiting for transfers between devices, last_partner(): return lax.ppermute(value, ('dp', 'expert'), pairs)  7.6 us
    pallas_call x2, Pallas kernels, first(): pl.pallas_call(functools.partial(first_kernel, replicas, flip), in_specs=...  7.21 us
    pallas_call x1, Pallas kernels, last(): pl.pallas_call(functools.partial(last_kernel, replicas), in_specs=[[in_vm...  7.09 us
    pallas_call x2, Pallas kernels, right(): pl.pallas_call(functools.partial(right_kernel, arrived.shape[1] // rank),...  2.85 us
    ppermute x2, starting transfers between devices, last_partner(): return lax.ppermute(value, ('dp', 'expert'), pairs)  2.51 us
  transfers between devices with their start and end apart: 12, of which 8 were waited for; matrix products, arithmetic and copies ran while one was open for 0% of the time, Pallas kernels for 4%

profile of v1, /device:TPU:0, one launch (start us, length us, event | category | flops | bytes accessed | tf_op | source)
XLA Modules:
  0.0 89.5 jit_solution(5647262863505962906)
XLA Ops:
  0.6 3.6 %compensate_and_left.2 = (bf16[2048,768]{1,0:T(8,128)(2,1)S(1)}, bf16[4,128,128]{2,1,0:T(8,128)(2,1)S(1)}) custom-call(bf16[4096,768]{1,0:T(8,128)(2,1)} %bitcast.23, bf16[4096,768]{1,0:T(8,128)(2,1)} %bitcast.25, f32[32,768]{1,0:T(8,128)} %bitcast.27), custom_call_target="tpu_custom_call" | custom-call | flops 100663296 | bytes 6291456 | tf_op jit(solution)/shard_map/compensate_and_left/pallas_call | solution.py:93
  4.2 3.0 %collective-permute-start = (bf16[4,128,128]{2,1,0:T(8,128)(2,1)S(1)}, bf16[4,128,128]{2,1,0:T(8,128)(2,1)S(1)}, u32[]{:S(2)}, u32[]{:S(2)}) collective-permute-start(bf16[4,128,128]{2,1,0:T(8,128)(2,1)S(1)} %get-tuple-element.12), channel_id=1, source_target_pairs={{0,4},{4,0},{8,12},{12,8},{16,20},{20,16},{24,28},{28,24},{1,5},{5... | collective-permute-start | bytes 393224 | tf_op jit(solution)/shard_map/ppermute | solution.py:116
  7.3 3.6 %compensate_and_left.3 = (bf16[2048,768]{1,0:T(8,128)(2,1)S(1)}, bf16[4,128,128]{2,1,0:T(8,128)(2,1)S(1)}) custom-call(bf16[4096,768]{1,0:T(8,128)(2,1)} %bitcast.24, bf16[4096,768]{1,0:T(8,128)(2,1)} %bitcast.26, f32[32,768]{1,0:T(8,128)} %bitcast.28), custom_call_target="tpu_custom_call" | custom-call | flops 100663296 | bytes 6291456 | tf_op jit(solution)/shard_map/compensate_and_left/pallas_call | solution.py:93
  10.9 0.0 copy-start
  10.9 0.0 collective-permute-done
  10.9 1.8 %collective-permute-start.1 = (bf16[128,128]{1,0:T(8,128)(2,1)S(1)}, bf16[128,128]{1,0:T(8,128)(2,1)S(1)}, u32[]{:S(2)}, u32[]{:S(2)}) collective-permute-start(bf16[128,128]{1,0:T(8,128)(2,1)S(1)} %get-tuple-element.21), channel_id=1, source_target_pairs={{0,8},{4,12},{8,0},{12,4},{16,24},{20,28},{24,16},{28,20},{1,9},{5... | collective-permute-start | bytes 98312 | tf_op jit(solution)/shard_map/ppermute | solution.py:116
  12.7 2.5 %collective-permute-start.3 = (bf16[128,128]{1,0:T(8,128)(2,1)S(1)}, bf16[128,128]{1,0:T(8,128)(2,1)S(1)}, u32[]{:S(2)}, u32[]{:S(2)}) collective-permute-start(bf16[128,128]{1,0:T(8,128)(2,1)S(1)} %get-tuple-element.22), channel_id=1, source_target_pairs={{0,24},{4,28},{8,16},{12,20},{16,8},{20,12},{24,0},{28,4},{1,25},{... | collective-permute-start | bytes 98312 | tf_op jit(solution)/shard_map/ppermute | solution.py:116
  15.1 0.1 collective-permute-start.2
  15.3 0.0 collective-permute-done.1
  15.3 3.2 %collective-permute-done.3 = bf16[128,128]{1,0:T(8,128)(2,1)S(1)} collective-permute-done((bf16[128,128]{1,0:T(8,128)(2,1)S(1)}, bf16[128,128]{1,0:T(8,128)(2,1)S(1)}, u32[]{:S(2)}, u32[]{:S(2)}) %collective-permute-start.3) | collective-permute-done | bytes 32800 | tf_op jit(solution)/shard_map/ppermute | solution.py:116
  18.4 1.9 %collective-permute-done.2 = bf16[128,128]{1,0:T(8,128)(2,1)S(1)} collective-permute-done((bf16[128,128]{1,0:T(8,128)(2,1)S(1)}, bf16[128,128]{1,0:T(8,128)(2,1)S(1)}, u32[]{:S(2)}, u32[]{:S(2)}) %collective-permute-start.2) | collective-permute-done | bytes 32800 | tf_op jit(solution)/shard_map/ppermute | solution.py:116
  20.4 11.5 %all_to_all.15.arrived = bf16[8,128,128]{2,1,0:T(8,128)(2,1)S(1)} all-to-all(bf16[8,128,128]{2,1,0:T(8,128)(2,1)S(1)} %broadcast_in_dim.9), channel_id=1, replica_groups=mesh['dp'=8,'expert'=4] {'dp'}, dimensions={0} | all-to-all | bytes 524288 | tf_op jit(solution)/shard_map/all_to_all | solution.py:18
  31.9 1.4 %orthogonalize_and_right.2 = bf16[32,768]{1,0:T(8,128)(2,1)S(1)} custom-call(bf16[8,128,128]{2,1,0:T(8,128)(2,1)S(1)} %all_to_all.15.arrived, bf16[2048,768]{1,0:T(8,128)(2,1)S(1)} %get-tuple-element.14.halves_0_, bf16[2048,768]{1,0:T(8,128)(2,1)S(1)} %get-tuple-element.15.halves_1_), custom_call_target="tpu_custom_call" | custom-call | tf_op jit(solution)/shard_map/orthogonalize_and_right/pallas_call | solution.py:203
  33.3 1.0 %collective-permute-start.6 = (bf16[32,768]{1,0:T(8,128)(2,1)S(1)}, bf16[32,768]{1,0:T(8,128)(2,1)S(1)}, u32[]{:S(2)}, u32[]{:S(2)}) collective-permute-start(bf16[32,768]{1,0:T(8,128)(2,1)S(1)} %orthogonalize_and_right.2), channel_id=1, source_target_pairs={{0,12},{4,8},{8,4},{12,0},{16,28},{20,24},{24,20},{28,16},{1,13},{... | collective-permute-start | bytes 147464 | tf_op jit(solution)/shard_map/ppermute | solution.py:116
  34.3 0.6 collective-permute-start.5
  34.8 2.0 %collective-permute-start.4 = (bf16[32,768]{1,0:T(8,128)(2,1)S(1)}, bf16[32,768]{1,0:T(8,128)(2,1)S(1)}, u32[]{:S(2)}, u32[]{:S(2)}) collective-permute-start(bf16[32,768]{1,0:T(8,128)(2,1)S(1)} %orthogonalize_and_right.2), channel_id=1, source_target_pairs={{0,4},{4,0},{8,12},{12,8},{16,20},{20,16},{24,28},{28,24},{1,5},{5... | collective-permute-start | bytes 147464 | tf_op jit(solution)/shard_map/ppermute | solution.py:116
  36.8 1.5 %collective-permute-done.6 = bf16[32,768]{1,0:T(8,128)(2,1)S(1)} collective-permute-done((bf16[32,768]{1,0:T(8,128)(2,1)S(1)}, bf16[32,768]{1,0:T(8,128)(2,1)S(1)}, u32[]{:S(2)}, u32[]{:S(2)}) %collective-permute-start.6) | collective-permute-done | bytes 49184 | tf_op jit(solution)/shard_map/ppermute | solution.py:116
  38.3 0.0 collective-permute-done.5
  38.4 0.6 collective-permute-done.4
  39.0 1.2 %collective-permute-start.7 = (bf16[32,768]{1,0:T(8,128)(2,1)S(1)}, bf16[32,768]{1,0:T(8,128)(2,1)S(1)}, u32[]{:S(2)}, u32[]{:S(2)}) collective-permute-start(bf16[32,768]{1,0:T(8,128)(2,1)S(1)} %add_convert_fusion.1.parts_0_), channel_id=1, source_target_pairs={{0,16},{1,25},{2,18},{3,27},{4,20},{5,29},{6,22},{7,31},{8,24},{9,... | collective-permute-start | bytes 147464 | tf_op jit(solution)/shard_map/ppermute | solution.py:220
  40.1 3.9 %collective-permute-done.7.parts_1_ = bf16[32,768]{1,0:T(8,128)(2,1)S(1)} collective-permute-done((bf16[32,768]{1,0:T(8,128)(2,1)S(1)}, bf16[32,768]{1,0:T(8,128)(2,1)S(1)}, u32[]{:S(2)}, u32[]{:S(2)}) %collective-permute-start.7) | collective-permute-done | bytes 49184 | tf_op jit(solution)/shard_map/ppermute | solution.py:220
  44.0 0.0 copy-done
  44.0 1.9 %normalize_and_left.1 = bf16[8,192,128]{2,1,0:T(8,128)(2,1)S(1)} custom-call(bf16[32,768]{1,0:T(8,128)(2,1)S(1)} %add_convert_fusion.1.parts_0_, bf16[32,768]{1,0:T(8,128)(2,1)S(1)} %collective-permute-done.7.parts_1_, bf16[2048,768]{1,0:T(8,128)(2,1)S(1)} %get-tuple-element.14.halves_0_, bf16[2048,768]{1,0:T(8,128)(2,1)S(1)} %get-tuple-element.15.halves_1_, ...), custom_call_target="tpu_custom_call" | custom-call | tf_op jit(solution)/shard_map/normalize_and_left/pallas_call | solution.py:265
  45.9 13.1 %all_to_all.16 = bf16[8,192,128]{2,1,0:T(8,128)(2,1)S(1)} all-to-all(bf16[8,192,128]{2,1,0:T(8,128)(2,1)S(1)} %normalize_and_left.1), channel_id=1, replica_groups=mesh['dp'=8,'expert'=4] {'dp'}, dimensions={0} | all-to-all | bytes 786432 | tf_op jit(solution)/shard_map/all_to_all | solution.py:18
  59.0 0.1 convert_reduce_fusion
  59.2 11.1 %all_to_all.17.arrived = bf16[8,128,128]{2,1,0:T(8,128)(2,1)S(1)} all-to-all(bf16[8,128,128]{2,1,0:T(8,128)(2,1)S(1)} %broadcast_in_dim.10), channel_id=1, replica_groups=mesh['dp'=8,'expert'=4] {'dp'}, dimensions={0} | all-to-all | bytes 524288 | tf_op jit(solution)/shard_map/all_to_all | solution.py:18
  70.2 1.4 %orthogonalize_and_right.3 = (bf16[32,768]{1,0:T(8,128)(2,1)S(1)}, f32[32,32]{1,0:T(8,128)S(1)}) custom-call(bf16[8,128,128]{2,1,0:T(8,128)(2,1)S(1)} %all_to_all.17.arrived, bf16[2048,768]{1,0:T(8,128)(2,1)S(1)} %get-tuple-element.14.halves_0_, bf16[2048,768]{1,0:T(8,128)(2,1)S(1)} %get-tuple-element.15.halves_1_), custom_call_target="tpu_custom_call" | custom-call | tf_op jit(solution)/shard_map/orthogonalize_and_right/pallas_call | solution.py:203
  71.7 1.0 %collective-permute-start.10 = (bf16[32,768]{1,0:T(8,128)(2,1)S(1)}, bf16[32,768]{1,0:T(8,128)(2,1)S(1)}, u32[]{:S(2)}, u32[]{:S(2)}) collective-permute-start(bf16[32,768]{1,0:T(8,128)(2,1)S(1)} %get-tuple-element.16), channel_id=1, source_target_pairs={{0,12},{4,8},{8,4},{12,0},{16,28},{20,24},{24,20},{28,16},{1,13},{... | collective-permute-start | bytes 147464 | tf_op jit(solution)/shard_map/ppermute | solution.py:116
  72.6 0.6 collective-permute-start.9
  73.2 2.0 %collective-permute-start.8 = (bf16[32,768]{1,0:T(8,128)(2,1)S(1)}, bf16[32,768]{1,0:T(8,128)(2,1)S(1)}, u32[]{:S(2)}, u32[]{:S(2)}) collective-permute-start(bf16[32,768]{1,0:T(8,128)(2,1)S(1)} %get-tuple-element.16), channel_id=1, source_target_pairs={{0,4},{4,0},{8,12},{12,8},{16,20},{20,16},{24,28},{28,24},{1,5},{5... | collective-permute-start | bytes 147464 | tf_op jit(solution)/shard_map/ppermute | solution.py:116
  75.2 1.5 %collective-permute-done.10 = bf16[32,768]{1,0:T(8,128)(2,1)S(1)} collective-permute-done((bf16[32,768]{1,0:T(8,128)(2,1)S(1)}, bf16[32,768]{1,0:T(8,128)(2,1)S(1)}, u32[]{:S(2)}, u32[]{:S(2)}) %collective-permute-start.10) | collective-permute-done | bytes 49184 | tf_op jit(solution)/shard_map/ppermute | solution.py:116
  76.7 0.0 collective-permute-done.9
  76.7 0.6 collective-permute-done.8
  77.3 1.3 %collective-permute-start.11 = (bf16[32,768]{1,0:T(8,128)(2,1)S(1)}, bf16[32,768]{1,0:T(8,128)(2,1)S(1)}, u32[]{:S(2)}, u32[]{:S(2)}) collective-permute-start(bf16[32,768]{1,0:T(8,128)(2,1)S(1)} %add_convert_fusion.parts_0_), channel_id=1, source_target_pairs={{0,16},{1,17},{2,18},{3,19},{4,20},{5,21},{6,22},{7,23},{8,24},{9,... | collective-permute-start | bytes 147464 | tf_op jit(solution)/shard_map/ppermute | solution.py:220
  78.7 3.7 %collective-permute-done.11.parts_1_ = bf16[32,768]{1,0:T(8,128)(2,1)S(1)} collective-permute-done((bf16[32,768]{1,0:T(8,128)(2,1)S(1)}, bf16[32,768]{1,0:T(8,128)(2,1)S(1)}, u32[]{:S(2)}, u32[]{:S(2)}) %collective-permute-start.11) | collective-permute-done | bytes 49184 | tf_op jit(solution)/shard_map/ppermute | solution.py:220
  82.4 7.1 %update_and_error.1 = (f32[4096,768]{1,0:T(8,128)}, bf16[4096,768]{1,0:T(8,128)(2,1)}, f32[64,128]{1,0:T(8,128)}) custom-call(bf16[32,768]{1,0:T(8,128)(2,1)S(1)} %add_convert_fusion.parts_0_, bf16[32,768]{1,0:T(8,128)(2,1)S(1)} %collective-permute-done.11.parts_1_, f32[32,32]{1,0:T(8,128)S(1)} %get-tuple-element.17.inverse, ...), custom_call_target="tpu_custom_call" | custom-call | tf_op jit(solution)/shard_map/update_and_error/pallas_call | solution.py:314
  (8 shorter events, 0.2 us)
Async XLA Ops:
  4.2 6.6 %collective-permute-start = (bf16[4,128,128]{2,1,0:T(8,128)(2,1)S(1)}, bf16[4,128,128]{2,1,0:T(8,128)(2,1)S(1)}, u32[]{:S(2)}, u32[]{:S(2)}) collective-permute-start(bf16[4,128,128]{2,1,0:T(8,128)(2,1)S(1)} %get-tuple-element.12), channel_id=1, source_target_pairs={{0,4},{4,0},{8,12},{12,8},{16,20},{20,16},{24,28},{28,24},{1,5},{5... | collective-permute-start | bytes 393224 | tf_op jit(solution)/shard_map/ppermute | solution.py:116
  10.9 33.2 %copy-start = (f32[1,65536]{1,0:T(1,128)S(1)}, f32[1,65536]{1,0:T(1,128)}, u32[]{:S(2)}) copy-start(f32[1,65536]{1,0:T(1,128)} %param.7) | copy-start | bytes 786436
  10.9 4.4 %collective-permute-start.1 = (bf16[128,128]{1,0:T(8,128)(2,1)S(1)}, bf16[128,128]{1,0:T(8,128)(2,1)S(1)}, u32[]{:S(2)}, u32[]{:S(2)}) collective-permute-start(bf16[128,128]{1,0:T(8,128)(2,1)S(1)} %get-tuple-element.21), channel_id=1, source_target_pairs={{0,8},{4,12},{8,0},{12,4},{16,24},{20,28},{24,16},{28,20},{1,9},{5... | collective-permute-start | bytes 98312 | tf_op jit(solution)/shard_map/ppermute | solution.py:116
  12.7 5.8 %collective-permute-start.3 = (bf16[128,128]{1,0:T(8,128)(2,1)S(1)}, bf16[128,128]{1,0:T(8,128)(2,1)S(1)}, u32[]{:S(2)}, u32[]{:S(2)}) collective-permute-start(bf16[128,128]{1,0:T(8,128)(2,1)S(1)} %get-tuple-element.22), channel_id=1, source_target_pairs={{0,24},{4,28},{8,16},{12,20},{16,8},{20,12},{24,0},{28,4},{1,25},{... | collective-permute-start | bytes 98312 | tf_op jit(solution)/shard_map/ppermute | solution.py:116
  15.1 5.2 %collective-permute-start.2 = (bf16[128,128]{1,0:T(8,128)(2,1)S(1)}, bf16[128,128]{1,0:T(8,128)(2,1)S(1)}, u32[]{:S(2)}, u32[]{:S(2)}) collective-permute-start(bf16[128,128]{1,0:T(8,128)(2,1)S(1)} %get-tuple-element.23), channel_id=1, source_target_pairs={{0,16},{4,20},{8,24},{12,28},{16,0},{20,4},{24,8},{28,12},{1,17},{... | collective-permute-start | bytes 98312 | tf_op jit(solution)/shard_map/ppermute | solution.py:116
  33.3 5.1 %collective-permute-start.6 = (bf16[32,768]{1,0:T(8,128)(2,1)S(1)}, bf16[32,768]{1,0:T(8,128)(2,1)S(1)}, u32[]{:S(2)}, u32[]{:S(2)}) collective-permute-start(bf16[32,768]{1,0:T(8,128)(2,1)S(1)} %orthogonalize_and_right.2), channel_id=1, source_target_pairs={{0,12},{4,8},{8,4},{12,0},{16,28},{20,24},{24,20},{28,16},{1,13},{... | collective-permute-start | bytes 147464 | tf_op jit(solution)/shard_map/ppermute | solution.py:116
  34.3 4.1 %collective-permute-start.5 = (bf16[32,768]{1,0:T(8,128)(2,1)S(1)}, bf16[32,768]{1,0:T(8,128)(2,1)S(1)}, u32[]{:S(2)}, u32[]{:S(2)}) collective-permute-start(bf16[32,768]{1,0:T(8,128)(2,1)S(1)} %orthogonalize_and_right.2), channel_id=1, source_target_pairs={{0,8},{4,12},{8,0},{12,4},{16,24},{20,28},{24,16},{28,20},{1,9},{5... | collective-permute-start | bytes 147464 | tf_op jit(solution)/shard_map/ppermute | solution.py:116
  34.8 4.1 %collective-permute-start.4 = (bf16[32,768]{1,0:T(8,128)(2,1)S(1)}, bf16[32,768]{1,0:T(8,128)(2,1)S(1)}, u32[]{:S(2)}, u32[]{:S(2)}) collective-permute-start(bf16[32,768]{1,0:T(8,128)(2,1)S(1)} %orthogonalize_and_right.2), channel_id=1, source_target_pairs={{0,4},{4,0},{8,12},{12,8},{16,20},{20,16},{24,28},{28,24},{1,5},{5... | collective-permute-start | bytes 147464 | tf_op jit(solution)/shard_map/ppermute | solution.py:116
  39.0 5.1 %collective-permute-start.7 = (bf16[32,768]{1,0:T(8,128)(2,1)S(1)}, bf16[32,768]{1,0:T(8,128)(2,1)S(1)}, u32[]{:S(2)}, u32[]{:S(2)}) collective-permute-start(bf16[32,768]{1,0:T(8,128)(2,1)S(1)} %add_convert_fusion.1.parts_0_), channel_id=1, source_target_pairs={{0,16},{1,25},{2,18},{3,27},{4,20},{5,29},{6,22},{7,31},{8,24},{9,... | collective-permute-start | bytes 147464 | tf_op jit(solution)/shard_map/ppermute | solution.py:220
  71.7 5.1 %collective-permute-start.10 = (bf16[32,768]{1,0:T(8,128)(2,1)S(1)}, bf16[32,768]{1,0:T(8,128)(2,1)S(1)}, u32[]{:S(2)}, u32[]{:S(2)}) collective-permute-start(bf16[32,768]{1,0:T(8,128)(2,1)S(1)} %get-tuple-element.16), channel_id=1, source_target_pairs={{0,12},{4,8},{8,4},{12,0},{16,28},{20,24},{24,20},{28,16},{1,13},{... | collective-permute-start | bytes 147464 | tf_op jit(solution)/shard_map/ppermute | solution.py:116
  72.6 4.1 %collective-permute-start.9 = (bf16[32,768]{1,0:T(8,128)(2,1)S(1)}, bf16[32,768]{1,0:T(8,128)(2,1)S(1)}, u32[]{:S(2)}, u32[]{:S(2)}) collective-permute-start(bf16[32,768]{1,0:T(8,128)(2,1)S(1)} %get-tuple-element.16), channel_id=1, source_target_pairs={{0,8},{4,12},{8,0},{12,4},{16,24},{20,28},{24,16},{28,20},{1,9},{5... | collective-permute-start | bytes 147464 | tf_op jit(solution)/shard_map/ppermute | solution.py:116
  73.2 4.1 %collective-permute-start.8 = (bf16[32,768]{1,0:T(8,128)(2,1)S(1)}, bf16[32,768]{1,0:T(8,128)(2,1)S(1)}, u32[]{:S(2)}, u32[]{:S(2)}) collective-permute-start(bf16[32,768]{1,0:T(8,128)(2,1)S(1)} %get-tuple-element.16), channel_id=1, source_target_pairs={{0,4},{4,0},{8,12},{12,8},{16,20},{20,16},{24,28},{28,24},{1,5},{5... | collective-permute-start | bytes 147464 | tf_op jit(solution)/shard_map/ppermute | solution.py:116
  77.3 5.1 %collective-permute-start.11 = (bf16[32,768]{1,0:T(8,128)(2,1)S(1)}, bf16[32,768]{1,0:T(8,128)(2,1)S(1)}, u32[]{:S(2)}, u32[]{:S(2)}) collective-permute-start(bf16[32,768]{1,0:T(8,128)(2,1)S(1)} %add_convert_fusion.parts_0_), channel_id=1, source_target_pairs={{0,16},{1,17},{2,18},{3,19},{4,20},{5,21},{6,22},{7,23},{8,24},{9,... | collective-permute-start | bytes 147464 | tf_op jit(solution)/shard_map/ppermute | solution.py:220

commit v2 on v1

--- a/solution.py
+++ b/solution.py
@@ -210,17 +210,17 @@
     )(arrived, halves)
 
 
-def last_partner(value, step, size, detour):
+def last_partner(value, step, size):
     experts = lax.axis_size("expert")
     pairs = []
     for i in range(size):
         for e in range(experts):
-            other = i ^ (step ^ 2 if detour and e % 2 else step)
+            other = i ^ (step ^ 2 if e % 2 else step)
             pairs.append((i * experts + e, other * experts + e))
     return lax.ppermute(value, ("dp", "expert"), pairs)
 
 
-def addends(term, size, detour):
+def addends(term, size):
     one, two, three, four = [
         part.astype(jnp.float32) for part in [term] + [partner(term, by, size) for by in (1, 2, 3)]
     ]
@@ -231,7 +231,7 @@
             jnp.bfloat16
         )
         step *= 2
-    return [term, last_partner(term, step, size, detour)]
+    return [term, last_partner(term, step, size)]
 
 
 def sum_of(parts):
@@ -344,7 +344,7 @@
         share = share / replicas
         factor_p = everywhere(share[:tall].astype(jnp.bfloat16), replicas)
         term, *inverse = right(factor_p, halves, rank, step + 1 == ITERS)
-        parts = addends(term, replicas, step + 1 < ITERS)
+        parts = addends(term, replicas)
         if step + 1 < ITERS:
             outgoing = left(parts, halves, bucket)
     update, new_error, bucket_mean = last(

time: 89.7 us -> 89.7 us (level)
  no operation moved by 1% of the time
where the time goes in v2:
time: 89.7 us; the launch traced here: 89.5 us
  blocking collectives  35.6 us (40%)
  Pallas kernels  19.1 us (21%)
  starting transfers between devices  17 us (19%)
  waiting for transfers between devices  16.8 us (19%)
    all_to_all x3, blocking collectives, exchange(): return lax.all_to_all(chunks, 'dp', split_axis=0, concat_axis=0, tiled=True)  35.6 us
    ppermute x10, starting transfers between devices, partner(): return lax.ppermute(value, 'dp', [(i, i ^ by) for i in range(size)])  14.5 us
    ppermute x10, waiting for transfers between devices, partner(): return lax.ppermute(value, 'dp', [(i, i ^ by) for i in range(size)])  9.2 us
    ppermute x2, waiting for transfers between devices, last_partner(): return lax.ppermute(value, ('dp', 'expert'), pairs)  7.6 us
    pallas_call x2, Pallas kernels, first(): pl.pallas_call(functools.partial(first_kernel, replicas, flip), in_specs=...  7.21 us
    pallas_call x1, Pallas kernels, last(): pl.pallas_call(functools.partial(last_kernel, replicas), in_specs=[[in_vm...  7.09 us
    pallas_call x2, Pallas kernels, right(): pl.pallas_call(functools.partial(right_kernel, arrived.shape[1] // rank),...  2.85 us
    ppermute x2, starting transfers between devices, last_partner(): return lax.ppermute(value, ('dp', 'expert'), pairs)  2.51 us
  transfers between devices with their start and end apart: 12, of which 8 were waited for; matrix products, arithmetic and copies ran while one was open for 0% of the time, Pallas kernels for 4%

profile of v2, /device:TPU:0, one launch (start us, length us, event | category | flops | bytes accessed | tf_op | source)
XLA Modules:
  0.0 89.5 jit_solution(14098567457632790777)
XLA Ops:
  0.6 3.6 %compensate_and_left.2 = (bf16[2048,768]{1,0:T(8,128)(2,1)S(1)}, bf16[4,128,128]{2,1,0:T(8,128)(2,1)S(1)}) custom-call(bf16[4096,768]{1,0:T(8,128)(2,1)} %bitcast.23, bf16[4096,768]{1,0:T(8,128)(2,1)} %bitcast.25, f32[32,768]{1,0:T(8,128)} %bitcast.27), custom_call_target="tpu_custom_call" | custom-call | flops 100663296 | bytes 6291456 | tf_op jit(solution)/shard_map/compensate_and_left/pallas_call | solution.py:93
  4.2 3.0 %collective-permute-start = (bf16[4,128,128]{2,1,0:T(8,128)(2,1)S(1)}, bf16[4,128,128]{2,1,0:T(8,128)(2,1)S(1)}, u32[]{:S(2)}, u32[]{:S(2)}) collective-permute-start(bf16[4,128,128]{2,1,0:T(8,128)(2,1)S(1)} %get-tuple-element.12), channel_id=1, source_target_pairs={{0,4},{4,0},{8,12},{12,8},{16,20},{20,16},{24,28},{28,24},{1,5},{5... | collective-permute-start | bytes 393224 | tf_op jit(solution)/shard_map/ppermute | solution.py:116
  7.3 3.6 %compensate_and_left.3 = (bf16[2048,768]{1,0:T(8,128)(2,1)S(1)}, bf16[4,128,128]{2,1,0:T(8,128)(2,1)S(1)}) custom-call(bf16[4096,768]{1,0:T(8,128)(2,1)} %bitcast.24, bf16[4096,768]{1,0:T(8,128)(2,1)} %bitcast.26, f32[32,768]{1,0:T(8,128)} %bitcast.28), custom_call_target="tpu_custom_call" | custom-call | flops 100663296 | bytes 6291456 | tf_op jit(solution)/shard_map/compensate_and_left/pallas_call | solution.py:93
  10.9 0.0 copy-start
  10.9 0.0 collective-permute-done
  10.9 1.8 %collective-permute-start.1 = (bf16[128,128]{1,0:T(8,128)(2,1)S(1)}, bf16[128,128]{1,0:T(8,128)(2,1)S(1)}, u32[]{:S(2)}, u32[]{:S(2)}) collective-permute-start(bf16[128,128]{1,0:T(8,128)(2,1)S(1)} %get-tuple-element.21), channel_id=1, source_target_pairs={{0,8},{4,12},{8,0},{12,4},{16,24},{20,28},{24,16},{28,20},{1,9},{5... | collective-permute-start | bytes 98312 | tf_op jit(solution)/shard_map/ppermute | solution.py:116
  12.7 2.5 %collective-permute-start.3 = (bf16[128,128]{1,0:T(8,128)(2,1)S(1)}, bf16[128,128]{1,0:T(8,128)(2,1)S(1)}, u32[]{:S(2)}, u32[]{:S(2)}) collective-permute-start(bf16[128,128]{1,0:T(8,128)(2,1)S(1)} %get-tuple-element.22), channel_id=1, source_target_pairs={{0,24},{4,28},{8,16},{12,20},{16,8},{20,12},{24,0},{28,4},{1,25},{... | collective-permute-start | bytes 98312 | tf_op jit(solution)/shard_map/ppermute | solution.py:116
  15.1 0.1 collective-permute-start.2
  15.3 0.0 collective-permute-done.1
  15.3 3.2 %collective-permute-done.3 = bf16[128,128]{1,0:T(8,128)(2,1)S(1)} collective-permute-done((bf16[128,128]{1,0:T(8,128)(2,1)S(1)}, bf16[128,128]{1,0:T(8,128)(2,1)S(1)}, u32[]{:S(2)}, u32[]{:S(2)}) %collective-permute-start.3) | collective-permute-done | bytes 32800 | tf_op jit(solution)/shard_map/ppermute | solution.py:116
  18.4 1.9 %collective-permute-done.2 = bf16[128,128]{1,0:T(8,128)(2,1)S(1)} collective-permute-done((bf16[128,128]{1,0:T(8,128)(2,1)S(1)}, bf16[128,128]{1,0:T(8,128)(2,1)S(1)}, u32[]{:S(2)}, u32[]{:S(2)}) %collective-permute-start.2) | collective-permute-done | bytes 32800 | tf_op jit(solution)/shard_map/ppermute | solution.py:116
  20.4 11.5 %all_to_all.15.arrived = bf16[8,128,128]{2,1,0:T(8,128)(2,1)S(1)} all-to-all(bf16[8,128,128]{2,1,0:T(8,128)(2,1)S(1)} %broadcast_in_dim.9), channel_id=1, replica_groups=mesh['dp'=8,'expert'=4] {'dp'}, dimensions={0} | all-to-all | bytes 524288 | tf_op jit(solution)/shard_map/all_to_all | solution.py:18
  31.9 1.4 %orthogonalize_and_right.2 = bf16[32,768]{1,0:T(8,128)(2,1)S(1)} custom-call(bf16[8,128,128]{2,1,0:T(8,128)(2,1)S(1)} %all_to_all.15.arrived, bf16[2048,768]{1,0:T(8,128)(2,1)S(1)} %get-tuple-element.14.halves_0_, bf16[2048,768]{1,0:T(8,128)(2,1)S(1)} %get-tuple-element.15.halves_1_), custom_call_target="tpu_custom_call" | custom-call | tf_op jit(solution)/shard_map/orthogonalize_and_right/pallas_call | solution.py:203
  33.3 1.0 %collective-permute-start.6 = (bf16[32,768]{1,0:T(8,128)(2,1)S(1)}, bf16[32,768]{1,0:T(8,128)(2,1)S(1)}, u32[]{:S(2)}, u32[]{:S(2)}) collective-permute-start(bf16[32,768]{1,0:T(8,128)(2,1)S(1)} %orthogonalize_and_right.2), channel_id=1, source_target_pairs={{0,12},{4,8},{8,4},{12,0},{16,28},{20,24},{24,20},{28,16},{1,13},{... | collective-permute-start | bytes 147464 | tf_op jit(solution)/shard_map/ppermute | solution.py:116
  34.3 0.6 collective-permute-start.5
  34.8 2.0 %collective-permute-start.4 = (bf16[32,768]{1,0:T(8,128)(2,1)S(1)}, bf16[32,768]{1,0:T(8,128)(2,1)S(1)}, u32[]{:S(2)}, u32[]{:S(2)}) collective-permute-start(bf16[32,768]{1,0:T(8,128)(2,1)S(1)} %orthogonalize_and_right.2), channel_id=1, source_target_pairs={{0,4},{4,0},{8,12},{12,8},{16,20},{20,16},{24,28},{28,24},{1,5},{5... | collective-permute-start | bytes 147464 | tf_op jit(solution)/shard_map/ppermute | solution.py:116
  36.8 1.5 %collective-permute-done.6 = bf16[32,768]{1,0:T(8,128)(2,1)S(1)} collective-permute-done((bf16[32,768]{1,0:T(8,128)(2,1)S(1)}, bf16[32,768]{1,0:T(8,128)(2,1)S(1)}, u32[]{:S(2)}, u32[]{:S(2)}) %collective-permute-start.6) | collective-permute-done | bytes 49184 | tf_op jit(solution)/shard_map/ppermute | solution.py:116
  38.3 0.0 collective-permute-done.5
  38.4 0.6 collective-permute-done.4
  39.0 1.2 %collective-permute-start.7 = (bf16[32,768]{1,0:T(8,128)(2,1)S(1)}, bf16[32,768]{1,0:T(8,128)(2,1)S(1)}, u32[]{:S(2)}, u32[]{:S(2)}) collective-permute-start(bf16[32,768]{1,0:T(8,128)(2,1)S(1)} %add_convert_fusion.1.parts_0_), channel_id=1, source_target_pairs={{0,16},{1,25},{2,18},{3,27},{4,20},{5,29},{6,22},{7,31},{8,24},{9,... | collective-permute-start | bytes 147464 | tf_op jit(solution)/shard_map/ppermute | solution.py:220
  40.1 3.9 %collective-permute-done.7.parts_1_ = bf16[32,768]{1,0:T(8,128)(2,1)S(1)} collective-permute-done((bf16[32,768]{1,0:T(8,128)(2,1)S(1)}, bf16[32,768]{1,0:T(8,128)(2,1)S(1)}, u32[]{:S(2)}, u32[]{:S(2)}) %collective-permute-start.7) | collective-permute-done | bytes 49184 | tf_op jit(solution)/shard_map/ppermute | solution.py:220
  44.0 0.0 copy-done
  44.0 1.9 %normalize_and_left.1 = bf16[8,192,128]{2,1,0:T(8,128)(2,1)S(1)} custom-call(bf16[32,768]{1,0:T(8,128)(2,1)S(1)} %add_convert_fusion.1.parts_0_, bf16[32,768]{1,0:T(8,128)(2,1)S(1)} %collective-permute-done.7.parts_1_, bf16[2048,768]{1,0:T(8,128)(2,1)S(1)} %get-tuple-element.14.halves_0_, bf16[2048,768]{1,0:T(8,128)(2,1)S(1)} %get-tuple-element.15.halves_1_, ...), custom_call_target="tpu_custom_call" | custom-call | tf_op jit(solution)/shard_map/normalize_and_left/pallas_call | solution.py:265
  45.9 13.1 %all_to_all.16 = bf16[8,192,128]{2,1,0:T(8,128)(2,1)S(1)} all-to-all(bf16[8,192,128]{2,1,0:T(8,128)(2,1)S(1)} %normalize_and_left.1), channel_id=1, replica_groups=mesh['dp'=8,'expert'=4] {'dp'}, dimensions={0} | all-to-all | bytes 786432 | tf_op jit(solution)/shard_map/all_to_all | solution.py:18
  59.0 0.1 convert_reduce_fusion
  59.2 11.1 %all_to_all.17.arrived = bf16[8,128,128]{2,1,0:T(8,128)(2,1)S(1)} all-to-all(bf16[8,128,128]{2,1,0:T(8,128)(2,1)S(1)} %broadcast_in_dim.10), channel_id=1, replica_groups=mesh['dp'=8,'expert'=4] {'dp'}, dimensions={0} | all-to-all | bytes 524288 | tf_op jit(solution)/shard_map/all_to_all | solution.py:18
  70.2 1.4 %orthogonalize_and_right.3 = (bf16[32,768]{1,0:T(8,128)(2,1)S(1)}, f32[32,32]{1,0:T(8,128)S(1)}) custom-call(bf16[8,128,128]{2,1,0:T(8,128)(2,1)S(1)} %all_to_all.17.arrived, bf16[2048,768]{1,0:T(8,128)(2,1)S(1)} %get-tuple-element.14.halves_0_, bf16[2048,768]{1,0:T(8,128)(2,1)S(1)} %get-tuple-element.15.halves_1_), custom_call_target="tpu_custom_call" | custom-call | tf_op jit(solution)/shard_map/orthogonalize_and_right/pallas_call | solution.py:203
  71.7 1.0 %collective-permute-start.10 = (bf16[32,768]{1,0:T(8,128)(2,1)S(1)}, bf16[32,768]{1,0:T(8,128)(2,1)S(1)}, u32[]{:S(2)}, u32[]{:S(2)}) collective-permute-start(bf16[32,768]{1,0:T(8,128)(2,1)S(1)} %get-tuple-element.16), channel_id=1, source_target_pairs={{0,12},{4,8},{8,4},{12,0},{16,28},{20,24},{24,20},{28,16},{1,13},{... | collective-permute-start | bytes 147464 | tf_op jit(solution)/shard_map/ppermute | solution.py:116
  72.6 0.6 collective-permute-start.9
  73.2 2.0 %collective-permute-start.8 = (bf16[32,768]{1,0:T(8,128)(2,1)S(1)}, bf16[32,768]{1,0:T(8,128)(2,1)S(1)}, u32[]{:S(2)}, u32[]{:S(2)}) collective-permute-start(bf16[32,768]{1,0:T(8,128)(2,1)S(1)} %get-tuple-element.16), channel_id=1, source_target_pairs={{0,4},{4,0},{8,12},{12,8},{16,20},{20,16},{24,28},{28,24},{1,5},{5... | collective-permute-start | bytes 147464 | tf_op jit(solution)/shard_map/ppermute | solution.py:116
  75.2 1.5 %collective-permute-done.10 = bf16[32,768]{1,0:T(8,128)(2,1)S(1)} collective-permute-done((bf16[32,768]{1,0:T(8,128)(2,1)S(1)}, bf16[32,768]{1,0:T(8,128)(2,1)S(1)}, u32[]{:S(2)}, u32[]{:S(2)}) %collective-permute-start.10) | collective-permute-done | bytes 49184 | tf_op jit(solution)/shard_map/ppermute | solution.py:116
  76.7 0.0 collective-permute-done.9
  76.7 0.6 collective-permute-done.8
  77.3 1.3 %collective-permute-start.11 = (bf16[32,768]{1,0:T(8,128)(2,1)S(1)}, bf16[32,768]{1,0:T(8,128)(2,1)S(1)}, u32[]{:S(2)}, u32[]{:S(2)}) collective-permute-start(bf16[32,768]{1,0:T(8,128)(2,1)S(1)} %add_convert_fusion.parts_0_), channel_id=1, source_target_pairs={{0,16},{1,25},{2,18},{3,27},{4,20},{5,29},{6,22},{7,31},{8,24},{9,... | collective-permute-start | bytes 147464 | tf_op jit(solution)/shard_map/ppermute | solution.py:220
  78.7 3.7 %collective-permute-done.11.parts_1_ = bf16[32,768]{1,0:T(8,128)(2,1)S(1)} collective-permute-done((bf16[32,768]{1,0:T(8,128)(2,1)S(1)}, bf16[32,768]{1,0:T(8,128)(2,1)S(1)}, u32[]{:S(2)}, u32[]{:S(2)}) %collective-permute-start.11) | collective-permute-done | bytes 49184 | tf_op jit(solution)/shard_map/ppermute | solution.py:220
  82.4 7.1 %update_and_error.1 = (f32[4096,768]{1,0:T(8,128)}, bf16[4096,768]{1,0:T(8,128)(2,1)}, f32[64,128]{1,0:T(8,128)}) custom-call(bf16[32,768]{1,0:T(8,128)(2,1)S(1)} %add_convert_fusion.parts_0_, bf16[32,768]{1,0:T(8,128)(2,1)S(1)} %collective-permute-done.11.parts_1_, f32[32,32]{1,0:T(8,128)S(1)} %get-tuple-element.17.inverse, ...), custom_call_target="tpu_custom_call" | custom-call | tf_op jit(solution)/shard_map/update_and_error/pallas_call | solution.py:314
  (8 shorter events, 0.2 us)
Async XLA Ops:
  4.2 6.6 %collective-permute-start = (bf16[4,128,128]{2,1,0:T(8,128)(2,1)S(1)}, bf16[4,128,128]{2,1,0:T(8,128)(2,1)S(1)}, u32[]{:S(2)}, u32[]{:S(2)}) collective-permute-start(bf16[4,128,128]{2,1,0:T(8,128)(2,1)S(1)} %get-tuple-element.12), channel_id=1, source_target_pairs={{0,4},{4,0},{8,12},{12,8},{16,20},{20,16},{24,28},{28,24},{1,5},{5... | collective-permute-start | bytes 393224 | tf_op jit(solution)/shard_map/ppermute | solution.py:116
  10.9 33.2 %copy-start = (f32[1,65536]{1,0:T(1,128)S(1)}, f32[1,65536]{1,0:T(1,128)}, u32[]{:S(2)}) copy-start(f32[1,65536]{1,0:T(1,128)} %param.7) | copy-start | bytes 786436
  10.9 4.4 %collective-permute-start.1 = (bf16[128,128]{1,0:T(8,128)(2,1)S(1)}, bf16[128,128]{1,0:T(8,128)(2,1)S(1)}, u32[]{:S(2)}, u32[]{:S(2)}) collective-permute-start(bf16[128,128]{1,0:T(8,128)(2,1)S(1)} %get-tuple-element.21), channel_id=1, source_target_pairs={{0,8},{4,12},{8,0},{12,4},{16,24},{20,28},{24,16},{28,20},{1,9},{5... | collective-permute-start | bytes 98312 | tf_op jit(solution)/shard_map/ppermute | solution.py:116
  12.7 5.8 %collective-permute-start.3 = (bf16[128,128]{1,0:T(8,128)(2,1)S(1)}, bf16[128,128]{1,0:T(8,128)(2,1)S(1)}, u32[]{:S(2)}, u32[]{:S(2)}) collective-permute-start(bf16[128,128]{1,0:T(8,128)(2,1)S(1)} %get-tuple-element.22), channel_id=1, source_target_pairs={{0,24},{4,28},{8,16},{12,20},{16,8},{20,12},{24,0},{28,4},{1,25},{... | collective-permute-start | bytes 98312 | tf_op jit(solution)/shard_map/ppermute | solution.py:116
  15.1 5.2 %collective-permute-start.2 = (bf16[128,128]{1,0:T(8,128)(2,1)S(1)}, bf16[128,128]{1,0:T(8,128)(2,1)S(1)}, u32[]{:S(2)}, u32[]{:S(2)}) collective-permute-start(bf16[128,128]{1,0:T(8,128)(2,1)S(1)} %get-tuple-element.23), channel_id=1, source_target_pairs={{0,16},{4,20},{8,24},{12,28},{16,0},{20,4},{24,8},{28,12},{1,17},{... | collective-permute-start | bytes 98312 | tf_op jit(solution)/shard_map/ppermute | solution.py:116
  33.3 5.1 %collective-permute-start.6 = (bf16[32,768]{1,0:T(8,128)(2,1)S(1)}, bf16[32,768]{1,0:T(8,128)(2,1)S(1)}, u32[]{:S(2)}, u32[]{:S(2)}) collective-permute-start(bf16[32,768]{1,0:T(8,128)(2,1)S(1)} %orthogonalize_and_right.2), channel_id=1, source_target_pairs={{0,12},{4,8},{8,4},{12,0},{16,28},{20,24},{24,20},{28,16},{1,13},{... | collective-permute-start | bytes 147464 | tf_op jit(solution)/shard_map/ppermute | solution.py:116
  34.3 4.1 %collective-permute-start.5 = (bf16[32,768]{1,0:T(8,128)(2,1)S(1)}, bf16[32,768]{1,0:T(8,128)(2,1)S(1)}, u32[]{:S(2)}, u32[]{:S(2)}) collective-permute-start(bf16[32,768]{1,0:T(8,128)(2,1)S(1)} %orthogonalize_and_right.2), channel_id=1, source_target_pairs={{0,8},{4,12},{8,0},{12,4},{16,24},{20,28},{24,16},{28,20},{1,9},{5... | collective-permute-start | bytes 147464 | tf_op jit(solution)/shard_map/ppermute | solution.py:116
  34.8 4.1 %collective-permute-start.4 = (bf16[32,768]{1,0:T(8,128)(2,1)S(1)}, bf16[32,768]{1,0:T(8,128)(2,1)S(1)}, u32[]{:S(2)}, u32[]{:S(2)}) collective-permute-start(bf16[32,768]{1,0:T(8,128)(2,1)S(1)} %orthogonalize_and_right.2), channel_id=1, source_target_pairs={{0,4},{4,0},{8,12},{12,8},{16,20},{20,16},{24,28},{28,24},{1,5},{5... | collective-permute-start | bytes 147464 | tf_op jit(solution)/shard_map/ppermute | solution.py:116
  39.0 5.1 %collective-permute-start.7 = (bf16[32,768]{1,0:T(8,128)(2,1)S(1)}, bf16[32,768]{1,0:T(8,128)(2,1)S(1)}, u32[]{:S(2)}, u32[]{:S(2)}) collective-permute-start(bf16[32,768]{1,0:T(8,128)(2,1)S(1)} %add_convert_fusion.1.parts_0_), channel_id=1, source_target_pairs={{0,16},{1,25},{2,18},{3,27},{4,20},{5,29},{6,22},{7,31},{8,24},{9,... | collective-permute-start | bytes 147464 | tf_op jit(solution)/shard_map/ppermute | solution.py:220
  71.7 5.1 %collective-permute-start.10 = (bf16[32,768]{1,0:T(8,128)(2,1)S(1)}, bf16[32,768]{1,0:T(8,128)(2,1)S(1)}, u32[]{:S(2)}, u32[]{:S(2)}) collective-permute-start(bf16[32,768]{1,0:T(8,128)(2,1)S(1)} %get-tuple-element.16), channel_id=1, source_target_pairs={{0,12},{4,8},{8,4},{12,0},{16,28},{20,24},{24,20},{28,16},{1,13},{... | collective-permute-start | bytes 147464 | tf_op jit(solution)/shard_map/ppermute | solution.py:116
  72.6 4.1 %collective-permute-start.9 = (bf16[32,768]{1,0:T(8,128)(2,1)S(1)}, bf16[32,768]{1,0:T(8,128)(2,1)S(1)}, u32[]{:S(2)}, u32[]{:S(2)}) collective-permute-start(bf16[32,768]{1,0:T(8,128)(2,1)S(1)} %get-tuple-element.16), channel_id=1, source_target_pairs={{0,8},{4,12},{8,0},{12,4},{16,24},{20,28},{24,16},{28,20},{1,9},{5... | collective-permute-start | bytes 147464 | tf_op jit(solution)/shard_map/ppermute | solution.py:116
  73.2 4.1 %collective-permute-start.8 = (bf16[32,768]{1,0:T(8,128)(2,1)S(1)}, bf16[32,768]{1,0:T(8,128)(2,1)S(1)}, u32[]{:S(2)}, u32[]{:S(2)}) collective-permute-start(bf16[32,768]{1,0:T(8,128)(2,1)S(1)} %get-tuple-element.16), channel_id=1, source_target_pairs={{0,4},{4,0},{8,12},{12,8},{16,20},{20,16},{24,28},{28,24},{1,5},{5... | collective-permute-start | bytes 147464 | tf_op jit(solution)/shard_map/ppermute | solution.py:116
  77.3 5.1 %collective-permute-start.11 = (bf16[32,768]{1,0:T(8,128)(2,1)S(1)}, bf16[32,768]{1,0:T(8,128)(2,1)S(1)}, u32[]{:S(2)}, u32[]{:S(2)}) collective-permute-start(bf16[32,768]{1,0:T(8,128)(2,1)S(1)} %add_convert_fusion.parts_0_), channel_id=1, source_target_pairs={{0,16},{1,25},{2,18},{3,27},{4,20},{5,29},{6,22},{7,31},{8,24},{9,... | collective-permute-start | bytes 147464 | tf_op jit(solution)/shard_map/ppermute | solution.py:220
